TPU v7x, 256 devices: a whole 4x4x8 slice. The times are simulated.
256 devices in a mesh: dp: 8 (over x, z_lo), ctx: 32 (over y, z_hi, core).
Axes of the slice: x: 4, y: 4, z: 8 (z_hi: 4, z_lo: 2; z = z_hi * 2 + z_lo), core: 2. Of those that a mesh axis runs over, the one named last changes fastest.
Arguments:
- queries: bfloat16 [32768, 8192], P(('dp', 'ctx')), may hold values from -16 to 16
- out_grad: bfloat16 [32768, 8192], P(('dp', 'ctx')), may hold values from -6 to 6
- enc_states: bfloat16 [3072, 1024], P(('dp', 'ctx')), may hold values from -8 to 8
- w_key: bfloat16 [1024, 8192], P('dp', 'ctx'), may hold values from -1 to 1
- w_value: bfloat16 [1024, 8192], P('dp', 'ctx'), may hold values from -0.1875 to 0.1875
- dec_segments: int32 [32768], P(('dp', 'ctx')), may hold values from 0 to 3, as said below
- enc_segments: int32 [3072], P(('dp', 'ctx')), may hold values from 0 to 3, as said below
Outputs:
- query_grad: bfloat16 [32768, 8192], P(('dp', 'ctx'))
- enc_grad: bfloat16 [3072, 1024], P(('dp', 'ctx'))
- w_key_grad: float32 [1024, 8192], P('dp', 'ctx')
- w_value_grad: float32 [1024, 8192], P('dp', 'ctx')
Inputs may be any that keep to these rules, and one draw needn't show every extreme that they name: `dec_segments`: within each pack the ids never fall along the tokens, and each of the 4 ids has one or more decoder tokens in the pack. `enc_segments`: within each pack the ids never fall along the tokens, and each of the 4 ids has two or more encoder tokens in the pack.
All inputs are finite; a program needn't handle non-finite values.
Results may differ from a plain program's by a relative error of at most 0.019.
Values may be sent and summed in bfloat16 or wider, within the bound.
No kernel may reach another device: no remote copies, remote signals or barrier semaphores. Data moves between devices by JAX's collectives and lax.ppermute only.
A program may use at most 64 MiB of HBM per device.

v0:
```python
import math
import jax
import jax.numpy as jnp
from jax import lax
from jax.sharding import PartitionSpec as P

HEAD_DIM = 128


def side_by_side(arrays, axis, dim, along):
    ends, at = ([], 0)
    for a in arrays[:-1]:
        at += a.shape[along]
        ends.append(at)
    both = jnp.concatenate(arrays, axis=along)
    return tuple(jnp.split(lax.all_gather(both, axis, axis=dim, tiled=True), ends, axis=along))


def sent_to_all(value, axis):
    size = lax.axis_size(axis)
    return lax.all_to_all(
        jnp.broadcast_to(value[None], (size, *value.shape)), axis, 0, 0, tiled=True
    )


def joined_along(pieces, dim):
    pieces = jnp.moveaxis(pieces, 0, dim)
    lengths = pieces.shape
    return pieces.reshape(*lengths[:dim], lengths[dim] * lengths[dim + 1], *lengths[dim + 2 :])


def gathered_copies(value, axis, dim):
    pieces = sent_to_all(value, axis)
    return joined_along(pieces, dim)


def split_up(value, dim, size):
    lengths = value.shape
    pieces = value.reshape(*lengths[:dim], size, lengths[dim] // size, *lengths[dim + 1 :])
    return jnp.moveaxis(pieces, dim, 0)


def sum_at_owner(value, axis, dim):
    pieces = split_up(value, dim, lax.axis_size(axis))
    arrived = lax.all_to_all(pieces, axis, split_axis=0, concat_axis=0, tiled=True)
    return arrived.astype(jnp.float32).sum(axis=0)


def in_one_piece(arrays, axis, dim, along):
    ends, at = ([], 0)
    for a in arrays[:-1]:
        at += a.shape[along]
        ends.append(at)
    both = jnp.concatenate(arrays, axis=along)
    return tuple(
        jnp.split(lax.psum_scatter(both, axis, scatter_dimension=dim, tiled=True), ends, axis=along)
    )


def attend(queries, out_grads, key_rows, value_rows, query_ids, key_ids):
    length, full_width = queries.shape
    key_count = key_rows.shape[0]
    head_count = full_width // HEAD_DIM
    group_size = min(head_count, 16)
    column_count = group_size * HEAD_DIM
    row_count = math.gcd(length, 1024)

    def head_group(number):
        column_start = number * column_count
        key_block = key_rows.reshape(key_count, group_size, HEAD_DIM)
        value_block = value_rows.reshape(key_count, group_size, HEAD_DIM)

        def query_block(totals, block_number):
            first_row = block_number * row_count
            query_part = lax.dynamic_slice(
                queries, (first_row, column_start), (row_count, column_count)
            ).reshape(row_count, group_size, HEAD_DIM)
            grad_part = lax.dynamic_slice(
                out_grads, (first_row, column_start), (row_count, column_count)
            ).reshape(row_count, group_size, HEAD_DIM)
            block_ids = lax.dynamic_slice_in_dim(query_ids, first_row, row_count, 0)
            allowed = block_ids[:, None] == key_ids[None, :]
            scores = jnp.einsum(
                "qhd,khd->hqk", query_part, key_block, preferred_element_type=jnp.float32
            )
            scores = jnp.where(allowed[None], scores, -jnp.inf)
            highest = jnp.max(scores, axis=2, keepdims=True)
            weights = jnp.exp(scores - highest)
            probability = weights / jnp.sum(weights, axis=2, keepdims=True)
            upstream = jnp.einsum(
                "qhd,khd->hqk", grad_part, value_block, preferred_element_type=jnp.float32
            )
            row_dot = jnp.sum(probability * upstream, axis=2, keepdims=True)
            score_grad = (probability * (upstream - row_dot)).astype(jnp.bfloat16)
            rounded = probability.astype(jnp.bfloat16)
            key_total = totals[0] + jnp.einsum(
                "hqk,qhd->khd", score_grad, query_part, preferred_element_type=jnp.float32
            )
            value_total = totals[1] + jnp.einsum(
                "hqk,qhd->khd", rounded, grad_part, preferred_element_type=jnp.float32
            )
            totals = (key_total, value_total)
            query_grad = jnp.einsum(
                "hqk,khd->qhd", score_grad, key_block, preferred_element_type=jnp.float32
            ).astype(jnp.bfloat16)
            return (totals, query_grad.reshape(row_count, column_count))

        zeros = jnp.zeros((key_count, group_size, HEAD_DIM), jnp.float32)
        totals, query_grads = lax.scan(
            query_block, (zeros, zeros), jnp.arange(length // row_count, dtype=jnp.int32)
        )
        results = ()
        results = results + (query_grads.reshape(length, column_count),)
        results = results + (
            totals[0].reshape(key_count, column_count),
            totals[1].reshape(key_count, column_count),
        )
        return results

    pieces = lax.map(head_group, jnp.arange(head_count // group_size, dtype=jnp.int32))
    return tuple(
        (jnp.moveaxis(piece, 0, 1).reshape(piece.shape[1], full_width) for piece in pieces)
    )


def body(queries, out_grad, enc_states, w_key, w_value, dec_segments, enc_segments):
    encoder, key_ids = (
        lax.all_gather(enc_states, "ctx", axis=0, tiled=True),
        lax.all_gather(enc_segments, "ctx", axis=0, tiled=True),
    )
    key_weight, value_weight = side_by_side((w_key, w_value), "dp", 0, 1)
    key_part = jnp.dot(encoder, key_weight, preferred_element_type=jnp.float32).astype(jnp.bfloat16)
    value_part = jnp.dot(encoder, value_weight, preferred_element_type=jnp.float32).astype(
        jnp.bfloat16
    )
    local_queries, local_grads = (
        lax.all_to_all(queries, "ctx", split_axis=1, concat_axis=0, tiled=True),
        lax.all_to_all(out_grad, "ctx", split_axis=1, concat_axis=0, tiled=True),
    )
    query_ids = gathered_copies(dec_segments, "ctx", 0)
    head_grad, key_grad, value_grad = attend(
        local_queries, local_grads, key_part, value_part, query_ids, key_ids
    )
    query_grad = lax.all_to_all(head_grad, "ctx", split_axis=0, concat_axis=1, tiled=True)
    key_round = key_grad.astype(jnp.bfloat16)
    value_round = value_grad.astype(jnp.bfloat16)
    across = (((1,), (1,)), ((), ()))
    partial_value = lax.dot_general(
        key_round, key_weight, across, preferred_element_type=jnp.float32
    )
    partial_value = partial_value + lax.dot_general(
        value_round, value_weight, across, preferred_element_type=jnp.float32
    )
    enc_grad = sum_at_owner(partial_value.astype(jnp.bfloat16), "ctx", 0).astype(jnp.bfloat16)
    down = (((0,), (0,)), ((), ()))
    key_term = lax.dot_general(encoder, key_round, down, preferred_element_type=jnp.float32)
    value_term = lax.dot_general(encoder, value_round, down, preferred_element_type=jnp.float32)
    w_key_grad, w_value_grad = tuple(
        (
            part.astype(jnp.float32)
            for part in in_one_piece(
                (key_term.astype(jnp.bfloat16), value_term.astype(jnp.bfloat16)), "dp", 0, 1
            )
        )
    )
    return (query_grad, enc_grad, w_key_grad, w_value_grad)


def solution(mesh):
    in_specs = (
        P(("dp", "ctx"), None),
        P(("dp", "ctx"), None),
        P(("dp", "ctx"), None),
        P("dp", "ctx"),
        P("dp", "ctx"),
        P(("dp", "ctx")),
        P(("dp", "ctx")),
    )
    out_specs = (P(("dp", "ctx"), None), P(("dp", "ctx"), None), P("dp", "ctx"), P("dp", "ctx"))
    return jax.shard_map(body, mesh=mesh, in_specs=in_specs, out_specs=out_specs, check_vma=False)
```

profile of v0, /device:TPU:8, one launch (start us, length us, event | category | flops | bytes accessed | tf_op | source)
XLA Modules:
  0.0 417.5 jit_solution(9430888007886917703)
XLA Ops:
  7.2 4.1 copy.68
  11.2 11.7 %all-to-all-start = ((bf16[128,32,256]{0,2,1:T(8,128)(2,1)}), bf16[128,32,256]{0,2,1:T(8,128)(2,1)S(1)}, u32[]{:S(2)}, u32[]{:S(2)}) async-start(bf16[128,32,256]{0,2,1:T(8,128)(2,1)} %bitcast.99), calls=%async_computation | async-start | bytes 4194304 | tf_op jit(solution)/shard_map/all_to_all | solution.py:137
  22.9 4.1 copy.70
  27.1 44.4 %all-to-all-done = bf16[128,32,256]{0,2,1:T(8,128)(2,1)S(1)} async-done(((bf16[128,32,256]{0,2,1:T(8,128)(2,1)}), bf16[128,32,256]{0,2,1:T(8,128)(2,1)S(1)}, u32[]{:S(2)}, u32[]{:S(2)}) %all-to-all-start) | async-done | bytes 2097184 | tf_op jit(solution)/shard_map/all_to_all | solution.py:137
  71.4 1.3 copy-done.4
  72.8 7.6 %all-to-all-start.2 = ((bf16[128,32,256]{0,2,1:T(8,128)(2,1)}), bf16[128,32,256]{0,2,1:T(8,128)(2,1)}, u32[]{:S(2)}, u32[]{:S(2)}) async-start(bf16[128,32,256]{0,2,1:T(8,128)(2,1)} %bitcast.97), calls=%async_computation.2 | async-start | bytes 4194304 | tf_op jit(solution)/shard_map/all_to_all | solution.py:138
  81.2 96.0 %all-gather = bf16[32,12,1024]{2,1,0:T(8,128)(2,1)S(1)} all-gather(bf16[1,12,1024]{2,1,0:T(8,128)(2,1)S(1)} %bitcast.108), channel_id=1, replica_groups=mesh['dp'=8,'ctx'=32] {'ctx'}, dimensions={0}, use_global_device_ids=true | all-gather | bytes 811008 | tf_op jit(solution)/shard_map/all_gather | solution.py:128
  177.5 0.7 dynamic-slice
  179.1 17.7 %all-reduce = s32[384]{0:T(512)S(1)} all-reduce(s32[384]{0:T(512)S(1)} %dynamic-update-slice), channel_id=1, replica_groups=mesh['dp'=8,'ctx'=32] {'ctx'}, use_global_device_ids=true, to_apply=%add | all-reduce | flops 384 | bytes 3072
  196.8 1.5 convolution_convert_fusion.3
  199.0 10.4 %all-to-all-start.1 = ((s32[32,1,128]{2,1,0:T(1,128)}), s32[32,1,128]{2,1,0:T(1,128)}, u32[]{:S(2)}, u32[]{:S(2)}) async-start(s32[32,1,128]{2,1,0:T(1,128)} %broadcast_in_dim.41), calls=%async_computation.1 | async-start | bytes 32768 | tf_op jit(solution)/shard_map/all_to_all | solution.py:21
  209.4 2.2 convolution_convert_fusion.4
  211.6 0.8 copy.74
  212.4 3.3 copy.69
  215.7 4.1 copy.71
  219.8 62.6 %while.27 = (s32[]{:T(128)}, f32[384,2,128]{0,2,1:T(8,128)S(1)}, f32[384,2,128]{0,2,1:T(8,128)}, bf16[4,1024,256]{2,1,0:T(8,128)(2,1)}, s32[4]{0:T(128)S(1)}, /*...) while((s32[]{:T(128)}, f32[384,2,128]{0,2,1:T(8,128)S(1)}, ...), condition=%wide.region_4.5_spmd.clone, body=%wide.region_0.4_spmd.clone.sunk | while | flops 1017117056 | bytes 58062732 | solution.py:109
  221.9 1.1 broadcast_compare_fusion.2
  222.9 1.1 constant_dynamic-slice_fusion.3
  224.1 1.0 copy.98
  225.1 1.0 copy.99
  226.1 2.5 fusion.69
  228.7 2.6 fusion.71
  231.8 0.8 multiply_convert_fusion.2
  234.4 0.8 constant_dynamic-update-slice_fusion.2
  236.7 0.7 dynamic_slice.33
  237.4 1.1 broadcast_compare_fusion.2
  238.5 1.1 constant_dynamic-slice_fusion.3
  239.6 1.0 copy.98
  240.6 1.0 copy.99
  241.6 2.5 fusion.69
  244.2 2.7 fusion.71
  247.5 0.8 multiply_convert_fusion.2
  250.1 0.8 constant_dynamic-update-slice_fusion.2
  252.4 0.7 dynamic_slice.33
  253.1 1.1 broadcast_compare_fusion.2
  254.2 1.1 constant_dynamic-slice_fusion.3
  255.3 1.0 copy.98
  256.3 1.0 copy.99
  257.3 2.5 fusion.69
  259.9 2.7 fusion.71
  263.2 0.8 multiply_convert_fusion.2
  265.8 0.8 constant_dynamic-update-slice_fusion.2
  268.1 0.7 dynamic_slice.33
  268.8 1.1 broadcast_compare_fusion.2
  269.9 1.1 constant_dynamic-slice_fusion.3
  271.0 1.0 copy.98
  272.0 1.0 copy.99
  273.0 2.5 fusion.69
  275.6 2.7 fusion.71
  278.8 0.8 multiply_convert_fusion.2
  281.4 0.8 constant_dynamic-update-slice_fusion.2
  282.4 1.1 convert_element_type.68
  283.5 1.5 fusion.22
  285.6 36.9 %all_to_all.68 = bf16[32,12,1024]{2,1,0:T(8,128)(2,1)} all-to-all(bf16[32,12,1024]{2,1,0:T(8,128)(2,1)S(1)} %reshape.98), channel_id=1, replica_groups=mesh['dp'=8,'ctx'=32] {'ctx'}, dimensions={0} | all-to-all | bytes 1572864 | tf_op jit(solution)/shard_map/all_to_all | solution.py:45
  322.5 6.9 %all-to-all-start.3 = ((bf16[32,128,256]{2,1,0:T(8,128)(2,1)}), bf16[32,128,256]{2,1,0:T(8,128)(2,1)S(1)}, u32[]{:S(2)}, u32[]{:S(2)}) async-start(bf16[32,128,256]{2,1,0:T(8,128)(2,1)} %bitcast.102), calls=%async_computation.3 | async-start | bytes 4194304 | tf_op jit(solution)/shard_map/all_to_all | solution.py:144
  330.4 1.0 pad_maximum_fusion
  331.5 2.4 copy.86
  333.9 0.8 reduce_sum.32
  334.7 66.3 %reduce-scatter.4.cloned.1.call-done = bf16[128,512]{1,0:T(8,128)(2,1)} async-done(((bf16[1024,512]{1,0:T(8,128)(2,1)}), bf16[128,512]{1,0:T(8,128)(2,1)}) %reduce-scatter.4.cloned.1.call-update) | async-done | bytes 131088
  401.0 0.9 fusion.26
  402.0 0.8 copy.79
  402.9 0.8 copy.78
  403.7 2.9 copy.76
  406.6 4.1 copy.77
  (114 shorter events, 17.0 us)
Async XLA Ops:
  11.2 60.2 %all-to-all-start = ((bf16[128,32,256]{0,2,1:T(8,128)(2,1)}), bf16[128,32,256]{0,2,1:T(8,128)(2,1)S(1)}, u32[]{:S(2)}, u32[]{:S(2)}) async-start(bf16[128,32,256]{0,2,1:T(8,128)(2,1)} %bitcast.99), calls=%async_computation | async-start | bytes 4194304 | tf_op jit(solution)/shard_map/all_to_all | solution.py:137
  71.4 1.3 copy-start.4
  71.4 9.0 %copy-start.11 = (bf16[128,256]{1,0:T(8,128)(2,1)S(1)}, bf16[128,256]{1,0:T(8,128)(2,1)}, u32[]{:S(2)}) copy-start(bf16[128,256]{1,0:T(8,128)(2,1)} %param.13) | copy-start | bytes 196612
  71.4 9.1 %copy-start.12 = (bf16[128,256]{1,0:T(8,128)(2,1)S(1)}, bf16[128,256]{1,0:T(8,128)(2,1)}, u32[]{:S(2)}) copy-start(bf16[128,256]{1,0:T(8,128)(2,1)} %param.12) | copy-start | bytes 196612
  71.4 9.8 %copy-start.13 = (bf16[12,1024]{1,0:T(8,128)(2,1)S(1)}, bf16[12,1024]{1,0:T(8,128)(2,1)}, u32[]{:S(2)}) copy-start(bf16[12,1024]{1,0:T(8,128)(2,1)} %param.11) | copy-start | bytes 73732
  72.8 125.6 %all-to-all-start.2 = ((bf16[128,32,256]{0,2,1:T(8,128)(2,1)}), bf16[128,32,256]{0,2,1:T(8,128)(2,1)}, u32[]{:S(2)}, u32[]{:S(2)}) async-start(bf16[128,32,256]{0,2,1:T(8,128)(2,1)} %bitcast.97), calls=%async_computation.2 | async-start | bytes 4194304 | tf_op jit(solution)/shard_map/all_to_all | solution.py:138
  80.4 97.1 %copy-start.16 = (u32[256]{0:T(256)S(1)}, u32[256]{0:T(256)}, u32[]{:S(2)}) copy-start(u32[256]{0:T(256)} %constant.64) | copy-start | bytes 3076
  80.4 98.4 %copy-start.15 = (s32[12]{0:T(128)S(1)}, s32[12]{0:T(128)}, u32[]{:S(2)}) copy-start(s32[12]{0:T(128)} %param.15) | copy-start | bytes 148
  80.4 116.4 %all-gather.3.cloned.1.call-start = ((), (), s32[]{:S(2)}) async-start(), calls=%async_computation.6 | async-start | bytes 1179648 | tf_op jit(solution)/shard_map/all_gather | solution.py:16
  81.2 117.1 %copy-start.14 = (s32[128]{0:T(128)S(1)}, s32[128]{0:T(128)}, u32[]{:S(2)}) copy-start(s32[128]{0:T(128)} %param.14) | copy-start | bytes 1540
  177.5 38.2 %copy-start.5 = (bf16[384,1024]{1,0:T(8,128)(2,1)}, bf16[384,1024]{1,0:T(8,128)(2,1)S(1)}, u32[]{:S(2)}) copy-start(bf16[384,1024]{1,0:T(8,128)(2,1)S(1)} %reshape.103) | copy-start | bytes 2359300
  199.0 20.8 %all-to-all-start.1 = ((s32[32,1,128]{2,1,0:T(1,128)}), s32[32,1,128]{2,1,0:T(1,128)}, u32[]{:S(2)}, u32[]{:S(2)}) async-start(s32[32,1,128]{2,1,0:T(1,128)} %broadcast_in_dim.41), calls=%async_computation.1 | async-start | bytes 32768 | tf_op jit(solution)/shard_map/all_to_all | solution.py:21
  219.8 6.3 %copy-start.2 = (bf16[4096,256]{1,0:T(8,128)(2,1)}, bf16[4096,256]{1,0:T(8,128)(2,1)S(1)}, u32[]{:S(2)}) copy-start(bf16[4096,256]{1,0:T(8,128)(2,1)S(1)} %get-tuple-element.377) | copy-start | bytes 6291460 | tf_op jit(solution)/shard_map/while/body/eval_jaxpr/while
  228.6 2.6 copy-start.1
  228.6 2.6 copy-start.10
  231.8 1.0 copy-start
  232.8 0.9 copy-start.7
  233.8 1.6 copy-start.3
  235.4 6.3 %copy-start.2 = (bf16[4096,256]{1,0:T(8,128)(2,1)}, bf16[4096,256]{1,0:T(8,128)(2,1)S(1)}, u32[]{:S(2)}) copy-start(bf16[4096,256]{1,0:T(8,128)(2,1)S(1)} %get-tuple-element.377) | copy-start | bytes 6291460 | tf_op jit(solution)/shard_map/while/body/eval_jaxpr/while
  244.2 2.7 copy-start.1
  244.2 2.7 copy-start.10
  247.5 1.0 copy-start
  248.5 0.9 copy-start.7
  249.4 1.6 copy-start.3
  251.0 6.3 %copy-start.2 = (bf16[4096,256]{1,0:T(8,128)(2,1)}, bf16[4096,256]{1,0:T(8,128)(2,1)S(1)}, u32[]{:S(2)}) copy-start(bf16[4096,256]{1,0:T(8,128)(2,1)S(1)} %get-tuple-element.377) | copy-start | bytes 6291460 | tf_op jit(solution)/shard_map/while/body/eval_jaxpr/while
  259.9 2.7 copy-start.1
  259.9 2.7 copy-start.10
  263.2 1.0 copy-start
  264.2 0.9 copy-start.7
  265.1 1.6 copy-start.3
  266.7 6.3 %copy-start.2 = (bf16[4096,256]{1,0:T(8,128)(2,1)}, bf16[4096,256]{1,0:T(8,128)(2,1)S(1)}, u32[]{:S(2)}) copy-start(bf16[4096,256]{1,0:T(8,128)(2,1)S(1)} %get-tuple-element.377) | copy-start | bytes 6291460 | tf_op jit(solution)/shard_map/while/body/eval_jaxpr/while
  275.5 2.7 copy-start.1
  275.6 2.7 copy-start.10
  278.8 1.0 copy-start
  279.9 0.9 copy-start.7
  280.8 1.6 copy-start.3
  282.4 2.6 copy-start.9
  322.5 7.0 %copy-start.6 = (bf16[384,1024]{1,0:T(8,128)(2,1)S(1)}, bf16[384,1024]{1,0:T(8,128)(2,1)}, u32[]{:S(2)}) copy-start(bf16[384,1024]{1,0:T(8,128)(2,1)} %copy-done.5) | copy-start | bytes 2359300
  322.5 81.2 %all-to-all-start.3 = ((bf16[32,128,256]{2,1,0:T(8,128)(2,1)}), bf16[32,128,256]{2,1,0:T(8,128)(2,1)S(1)}, u32[]{:S(2)}, u32[]{:S(2)}) async-start(bf16[32,128,256]{2,1,0:T(8,128)(2,1)} %bitcast.102), calls=%async_computation.3 | async-start | bytes 4194304 | tf_op jit(solution)/shard_map/all_to_all | solution.py:144
  329.5 71.6 %reduce-scatter.4.cloned.1.call-start = ((), (), s32[]{:S(2)}) async-start(), calls=%async_computation.7 | async-start | bytes 1179648
  331.5 2.4 copy-start.8
Sparse Core Ops, SparseCore 0:
  83.6 70.4 all-gather.2
  334.0 66.9 reduce-scatter.3
where the time goes:
time: 419 us; the launch traced here: 417 us
  blocking collectives  151 us (36%)
  waiting for transfers between devices  111 us (26%)
  local copies, waits for them, and re-layouts  56.4 us (13%)
  starting transfers between devices  36.7 us (9%)
  matrix products  33.8 us (8%)
  between operations  15 us (4%)
  other arithmetic  11.1 us (3%)
    all_gather x1, blocking collectives, body(): lax.all_gather(enc_states, 'ctx', axis=0, tiled=True)  96 us
    unnamed x3, waiting for transfers between devices  66.4 us
    all_to_all x1, waiting for transfers between devices, body(): lax.all_to_all(queries, 'ctx', split_axis=1, concat_axis=0, tiled=True)  44.4 us
    all_to_all x1, blocking collectives, sum_at_owner(): lax.all_to_all(pieces, axis, split_axis=0, concat_axis=0, tiled=True)  36.9 us
    unnamed x35, local copies, waits for them, and re-layouts  19.7 us
    unnamed x1, blocking collectives  17.7 us
    all_to_all x1, starting transfers between devices, body(): lax.all_to_all(queries, 'ctx', split_axis=1, concat_axis=0, tiled=True)  11.7 us
    dot_general x4, matrix products, query_block(): jnp.einsum('hqk,qhd->khd', rounded, grad_part, preferred_element_type=jnp...  10.5 us
  transfers between devices with their start and end apart: 6, of which 2 were waited for; matrix products, arithmetic and copies ran while one was open for 6% of the time, Pallas kernels for 0%

commit v1 on v0

--- a/solution.py
+++ b/solution.py
@@ -5,6 +5,13 @@
 from jax.sharding import PartitionSpec as P
 
 HEAD_DIM = 128
+
+
+def trade_parts(block, mesh_axis, split, join):
+    size = lax.axis_size(mesh_axis)
+    pieces = jnp.stack(jnp.split(block, size, axis=split), axis=0)
+    pieces = lax.all_to_all(pieces, mesh_axis, split_axis=0, concat_axis=0)
+    return jnp.concatenate(pieces, axis=join)
 
 
 def side_by_side(arrays, axis, dim, along):
@@ -135,7 +142,7 @@
     )
     local_queries, local_grads = (
         lax.all_to_all(queries, "ctx", split_axis=1, concat_axis=0, tiled=True),
-        lax.all_to_all(out_grad, "ctx", split_axis=1, concat_axis=0, tiled=True),
+        trade_parts(out_grad, "ctx", 1, 0),
     )
     query_ids = gathered_copies(dec_segments, "ctx", 0)
     head_grad, key_grad, value_grad = attend(

time: 419 us -> 446 us (1.064)
  local copies, waits for them, and re-layouts: 56.4 us -> 98.2 us
  waiting for transfers between devices: 111 us -> 87.8 us
    unnamed x35 -> x57, local copies, waits for them, and re-layouts: 19.7 us -> 62.3 us
    all_to_all x1, waiting for transfers between devices: 44.4 us -> 22 us  [body(): lax.all_to_all(queries, 'ctx', split_axis=1, concat_axis=0, tiled=True)]
  transfers between devices with their start and end apart: 6 -> 6, of which waited for: 2 -> 2; matrix products, arithmetic and copies ran while one was open for 6% -> 16% of each run, Pallas kernels for 0% -> 0%
where the time goes in v1:
time: 446 us; the launch traced here: 442 us
  blocking collectives  154 us (35%)
  local copies, waits for them, and re-layouts  98.2 us (22%)
  waiting for transfers between devices  87.8 us (20%)
  starting transfers between devices  36 us (8%)
  matrix products  33.8 us (8%)
  between operations  14.9 us (3%)
  other arithmetic  14.7 us (3%)
    all_gather x1, blocking collectives, body(): lax.all_gather(enc_states, 'ctx', axis=0, tiled=True)  98.6 us
    unnamed x3, waiting for transfers between devices  65.9 us
    unnamed x57, local copies, waits for them, and re-layouts  62.3 us
    all_to_all x1, blocking collectives, sum_at_owner(): lax.all_to_all(pieces, axis, split_axis=0, concat_axis=0, tiled=True)  37.2 us
    all_to_all x1, waiting for transfers between devices, body(): lax.all_to_all(queries, 'ctx', split_axis=1, concat_axis=0, tiled=True)  22 us
    unnamed x1, blocking collectives  17.9 us
    all_to_all x1, starting transfers between devices, sent_to_all(): lax.all_to_all(jnp.broadcast_to(value[None], (size, *value.shape)), axis,...  11.7 us
    dot_general x4, matrix products, query_block(): jnp.einsum('hqk,qhd->khd', rounded, grad_part, preferred_element_type=jnp...  10.4 us
  transfers between devices with their start and end apart: 6, of which 2 were waited for; matrix products, arithmetic and copies ran while one was open for 16% of the time, Pallas kernels for 0%

profile of v1, /device:TPU:8, one launch (start us, length us, event | category | flops | bytes accessed | tf_op | source)
XLA Modules:
  0.0 442.2 jit_solution(5791476317525853190)
XLA Ops:
  8.4 11.7 %all-to-all-start.1 = ((s32[32,1,128]{2,1,0:T(1,128)}), s32[32,1,128]{2,1,0:T(1,128)S(1)}, u32[]{:S(2)}, u32[]{:S(2)}) async-start(s32[32,1,128]{2,1,0:T(1,128)} %broadcast_in_dim.41), calls=%async_computation.1 | async-start | bytes 32768 | tf_op jit(solution)/shard_map/all_to_all | solution.py:28
  20.1 1.5 constant_dynamic-update-slice_fusion.32
  21.6 1.5 constant_dynamic-update-slice_fusion.31
  23.1 1.5 constant_dynamic-update-slice_fusion.30
  24.6 1.5 constant_dynamic-update-slice_fusion.29
  26.0 1.5 constant_dynamic-update-slice_fusion.28
  27.5 1.5 constant_dynamic-update-slice_fusion.27
  29.0 1.5 constant_dynamic-update-slice_fusion.26
  30.4 1.5 constant_dynamic-update-slice_fusion.25
  31.9 1.5 constant_dynamic-update-slice_fusion.24
  33.4 1.5 constant_dynamic-update-slice_fusion.23
  34.8 1.5 constant_dynamic-update-slice_fusion.22
  36.3 1.5 constant_dynamic-update-slice_fusion.21
  37.8 1.5 constant_dynamic-update-slice_fusion.20
  39.3 1.5 constant_dynamic-update-slice_fusion.19
  40.7 4.1 copy.67
  44.8 9.8 %all-to-all-start = ((bf16[128,32,256]{0,2,1:T(8,128)(2,1)}), bf16[128,32,256]{0,2,1:T(8,128)(2,1)S(1)}, u32[]{:S(2)}, u32[]{:S(2)}) async-start(bf16[128,32,256]{0,2,1:T(8,128)(2,1)} %bitcast.159), calls=%async_computation | async-start | bytes 4194304 | tf_op jit(solution)/shard_map/all_to_all | solution.py:144
  54.6 1.5 constant_dynamic-update-slice_fusion.18
  56.1 1.5 constant_dynamic-update-slice_fusion.17
  57.5 1.5 constant_dynamic-update-slice_fusion.16
  59.0 1.5 constant_dynamic-update-slice_fusion.15
  60.5 1.5 constant_dynamic-update-slice_fusion.14
  62.0 1.5 constant_dynamic-update-slice_fusion.13
  63.4 1.5 constant_dynamic-update-slice_fusion.12
  64.9 1.5 constant_dynamic-update-slice_fusion.11
  66.4 1.5 constant_dynamic-update-slice_fusion.10
  67.8 1.5 constant_dynamic-update-slice_fusion.9
  69.3 1.5 constant_dynamic-update-slice_fusion.8
  70.8 1.5 constant_dynamic-update-slice_fusion.7
  72.3 1.5 constant_dynamic-update-slice_fusion.6
  73.7 1.5 constant_dynamic-update-slice_fusion.5
  75.2 1.5 constant_dynamic-update-slice_fusion.4
  76.7 1.5 constant_dynamic-update-slice_fusion.3
  78.2 1.5 constant_dynamic-update-slice_fusion.2
  79.6 1.5 constant_dynamic-update-slice_fusion.1
  81.1 22.0 %all-to-all-done = bf16[128,32,256]{0,2,1:T(8,128)(2,1)S(1)} async-done(((bf16[128,32,256]{0,2,1:T(8,128)(2,1)}), bf16[128,32,256]{0,2,1:T(8,128)(2,1)S(1)}, u32[]{:S(2)}, u32[]{:S(2)}) %all-to-all-start) | async-done | bytes 2097184 | tf_op jit(solution)/shard_map/all_to_all | solution.py:144
  103.1 1.3 copy-done.4
  104.4 7.6 %all-to-all-start.2 = ((bf16[32,128,256]{2,1,0:T(8,128)(2,1)}), bf16[32,128,256]{2,1,0:T(8,128)(2,1)S(1)}, u32[]{:S(2)}, u32[]{:S(2)}) async-start(bf16[32,128,256]{2,1,0:T(8,128)(2,1)} %constant_dynamic-update-slice_fusion.1), calls=%async_computation.2 | async-start | bytes 4194304 | tf_op jit(solution)/shard_map/all_to_all | solution.py:13
  112.1 1.5 pad_maximum_fusion.1
  113.7 98.6 %all-gather = bf16[32,12,1024]{2,1,0:T(8,128)(2,1)} all-gather(bf16[1,12,1024]{2,1,0:T(8,128)(2,1)} %bitcast.169), channel_id=1, replica_groups=mesh['dp'=8,'ctx'=32] {'ctx'}, dimensions={0}, use_global_device_ids=true | all-gather | bytes 811008 | tf_op jit(solution)/shard_map/all_gather | solution.py:135
  215.2 17.9 %all-reduce = s32[384]{0:T(512)} all-reduce(s32[384]{0:T(512)S(1)} %dynamic-update-slice), channel_id=1, replica_groups=mesh['dp'=8,'ctx'=32] {'ctx'}, use_global_device_ids=true, to_apply=%add | all-reduce | flops 384 | bytes 3072
  233.1 1.5 convolution_convert_fusion.3
  235.5 2.2 convolution_convert_fusion.4
  237.7 4.1 copy.68
  242.3 65.1 %while.27 = (s32[]{:T(128)}, f32[384,2,128]{0,2,1:T(8,128)S(1)}, f32[384,2,128]{0,2,1:T(8,128)}, bf16[4,1024,256]{2,1,0:T(8,128)(2,1)}, s32[4]{0:T(128)}, /*inde...) while((s32[]{:T(128)}, f32[384,2,128]{0,2,1:T(8,128)S(1)}, ...), condition=%wide.region_4.5_spmd.clone, body=%wide.region_0.4_spmd.clone.sunk | while | flops 1017117056 | bytes 58193860 | solution.py:116
  244.3 1.8 broadcast_compare_fusion.2
  249.2 2.5 fusion.69
  251.8 2.5 fusion.71
  260.5 1.8 broadcast_compare_fusion.2
  265.4 2.5 fusion.69
  268.0 2.6 fusion.71
  276.8 1.8 broadcast_compare_fusion.2
  281.8 2.5 fusion.69
  284.3 2.6 fusion.71
  293.2 1.8 broadcast_compare_fusion.2
  298.1 2.5 fusion.69
  300.6 2.6 fusion.71
  308.6 1.5 fusion.22
  310.6 37.2 %all_to_all.54 = bf16[32,12,1024]{2,1,0:T(8,128)(2,1)} all-to-all(bf16[32,12,1024]{2,1,0:T(8,128)(2,1)S(1)} %reshape.99), channel_id=1, replica_groups=mesh['dp'=8,'ctx'=32] {'ctx'}, dimensions={0} | all-to-all | bytes 1572864 | tf_op jit(solution)/shard_map/all_to_all | solution.py:52
  347.8 6.9 %all-to-all-start.3 = ((bf16[32,128,256]{2,1,0:T(8,128)(2,1)}), bf16[32,128,256]{2,1,0:T(8,128)(2,1)S(1)}, u32[]{:S(2)}, u32[]{:S(2)}) async-start(bf16[32,128,256]{2,1,0:T(8,128)(2,1)} %bitcast.162), calls=%async_computation.3 | async-start | bytes 4194304 | tf_op jit(solution)/shard_map/all_to_all | solution.py:151
  356.7 2.4 copy.84
  360.0 65.8 %reduce-scatter.4.cloned.1.call-done = bf16[128,512]{1,0:T(8,128)(2,1)} async-done(((bf16[1024,512]{1,0:T(8,128)(2,1)}), bf16[128,512]{1,0:T(8,128)(2,1)}) %reduce-scatter.4.cloned.1.call-update) | async-done | bytes 131088
  428.5 2.9 copy.73
  431.3 4.1 copy.74
  (152 shorter events, 46.4 us)
Async XLA Ops:
  8.4 36.4 %all-to-all-start.1 = ((s32[32,1,128]{2,1,0:T(1,128)}), s32[32,1,128]{2,1,0:T(1,128)S(1)}, u32[]{:S(2)}, u32[]{:S(2)}) async-start(s32[32,1,128]{2,1,0:T(1,128)} %broadcast_in_dim.41), calls=%async_computation.1 | async-start | bytes 32768 | tf_op jit(solution)/shard_map/all_to_all | solution.py:28
  44.8 58.3 %all-to-all-start = ((bf16[128,32,256]{0,2,1:T(8,128)(2,1)}), bf16[128,32,256]{0,2,1:T(8,128)(2,1)S(1)}, u32[]{:S(2)}, u32[]{:S(2)}) async-start(bf16[128,32,256]{0,2,1:T(8,128)(2,1)} %bitcast.159), calls=%async_computation | async-start | bytes 4194304 | tf_op jit(solution)/shard_map/all_to_all | solution.py:144
  103.1 1.3 copy-start.4
  104.4 137.4 %all-to-all-start.2 = ((bf16[32,128,256]{2,1,0:T(8,128)(2,1)}), bf16[32,128,256]{2,1,0:T(8,128)(2,1)S(1)}, u32[]{:S(2)}, u32[]{:S(2)}) async-start(bf16[32,128,256]{2,1,0:T(8,128)(2,1)} %constant_dynamic-update-slice_fusion.1), calls=%async_computation.2 | async-start | bytes 4194304 | tf_op jit(solution)/shard_map/all_to_all | solution.py:13
  112.0 101.6 %copy-start.14 = (u32[256]{0:T(256)S(1)}, u32[256]{0:T(256)}, u32[]{:S(2)}) copy-start(u32[256]{0:T(256)} %constant.64) | copy-start | bytes 3076
  112.0 102.9 %copy-start.13 = (s32[12]{0:T(128)S(1)}, s32[12]{0:T(128)}, u32[]{:S(2)}) copy-start(s32[12]{0:T(128)} %param.15) | copy-start | bytes 148
  112.0 121.1 %all-gather.3.cloned.1.call-start = ((), (), s32[]{:S(2)}) async-start(), calls=%async_computation.6 | async-start | bytes 1179648 | tf_op jit(solution)/shard_map/all_gather | solution.py:23
  213.6 28.2 %copy-start.5 = (bf16[384,1024]{1,0:T(8,128)(2,1)}, bf16[384,1024]{1,0:T(8,128)(2,1)S(1)}, u32[]{:S(2)}) copy-start(bf16[384,1024]{1,0:T(8,128)(2,1)S(1)} %reshape.104) | copy-start | bytes 2359300
  242.3 6.9 %copy-start.2 = (bf16[4096,256]{1,0:T(8,128)(2,1)}, bf16[4096,256]{1,0:T(8,128)(2,1)S(1)}, u32[]{:S(2)}) copy-start(bf16[4096,256]{1,0:T(8,128)(2,1)S(1)} %get-tuple-element.381) | copy-start | bytes 6291460 | tf_op jit(solution)/shard_map/while/body/eval_jaxpr/while
  242.3 6.9 %copy-start.11 = (s32[4096]{0:T(1024)}, s32[4096]{0:T(1024)S(1)}, u32[]{:S(2)}) copy-start(s32[4096]{0:T(1024)S(1)} %get-tuple-element.378) | copy-start | bytes 49156 | tf_op jit(solution)/shard_map/while/body/eval_jaxpr/while
  251.8 2.6 copy-start.1
  251.8 2.5 copy-start.10
  254.9 1.0 copy-start
  256.0 0.9 copy-start.7
  256.9 1.6 copy-start.3
  256.9 1.6 copy-start.12
  258.5 6.9 %copy-start.2 = (bf16[4096,256]{1,0:T(8,128)(2,1)}, bf16[4096,256]{1,0:T(8,128)(2,1)S(1)}, u32[]{:S(2)}) copy-start(bf16[4096,256]{1,0:T(8,128)(2,1)S(1)} %get-tuple-element.381) | copy-start | bytes 6291460 | tf_op jit(solution)/shard_map/while/body/eval_jaxpr/while
  258.5 6.9 %copy-start.11 = (s32[4096]{0:T(1024)}, s32[4096]{0:T(1024)S(1)}, u32[]{:S(2)}) copy-start(s32[4096]{0:T(1024)S(1)} %get-tuple-element.378) | copy-start | bytes 49156 | tf_op jit(solution)/shard_map/while/body/eval_jaxpr/while
  268.0 2.7 copy-start.1
  268.0 2.7 copy-start.10
  271.2 1.0 copy-start
  272.3 0.9 copy-start.7
  273.2 1.6 copy-start.3
  273.2 1.6 copy-start.12
  274.8 6.9 %copy-start.2 = (bf16[4096,256]{1,0:T(8,128)(2,1)}, bf16[4096,256]{1,0:T(8,128)(2,1)S(1)}, u32[]{:S(2)}) copy-start(bf16[4096,256]{1,0:T(8,128)(2,1)S(1)} %get-tuple-element.381) | copy-start | bytes 6291460 | tf_op jit(solution)/shard_map/while/body/eval_jaxpr/while
  274.8 6.9 %copy-start.11 = (s32[4096]{0:T(1024)}, s32[4096]{0:T(1024)S(1)}, u32[]{:S(2)}) copy-start(s32[4096]{0:T(1024)S(1)} %get-tuple-element.378) | copy-start | bytes 49156 | tf_op jit(solution)/shard_map/while/body/eval_jaxpr/while
  284.3 2.7 copy-start.1
  284.3 2.7 copy-start.10
  287.6 1.0 copy-start
  288.6 0.9 copy-start.7
  289.5 1.6 copy-start.3
  289.5 1.6 copy-start.12
  291.1 6.9 %copy-start.2 = (bf16[4096,256]{1,0:T(8,128)(2,1)}, bf16[4096,256]{1,0:T(8,128)(2,1)S(1)}, u32[]{:S(2)}) copy-start(bf16[4096,256]{1,0:T(8,128)(2,1)S(1)} %get-tuple-element.381) | copy-start | bytes 6291460 | tf_op jit(solution)/shard_map/while/body/eval_jaxpr/while
  291.1 6.9 %copy-start.11 = (s32[4096]{0:T(1024)}, s32[4096]{0:T(1024)S(1)}, u32[]{:S(2)}) copy-start(s32[4096]{0:T(1024)S(1)} %get-tuple-element.378) | copy-start | bytes 49156 | tf_op jit(solution)/shard_map/while/body/eval_jaxpr/while
  300.6 2.7 copy-start.1
  300.6 2.6 copy-start.10
  303.9 1.0 copy-start
  304.9 0.9 copy-start.7
  305.8 1.6 copy-start.3
  305.8 1.6 copy-start.12
  307.4 2.6 copy-start.9
  347.8 7.0 %copy-start.6 = (bf16[384,1024]{1,0:T(8,128)(2,1)S(1)}, bf16[384,1024]{1,0:T(8,128)(2,1)}, u32[]{:S(2)}) copy-start(bf16[384,1024]{1,0:T(8,128)(2,1)} %copy-done.5) | copy-start | bytes 2359300
  347.8 80.6 %all-to-all-start.3 = ((bf16[32,128,256]{2,1,0:T(8,128)(2,1)}), bf16[32,128,256]{2,1,0:T(8,128)(2,1)S(1)}, u32[]{:S(2)}, u32[]{:S(2)}) async-start(bf16[32,128,256]{2,1,0:T(8,128)(2,1)} %bitcast.162), calls=%async_computation.3 | async-start | bytes 4194304 | tf_op jit(solution)/shard_map/all_to_all | solution.py:151
  354.7 71.1 %reduce-scatter.4.cloned.1.call-start = ((), (), s32[]{:S(2)}) async-start(), calls=%async_computation.7 | async-start | bytes 1179648
  356.7 2.4 copy-start.8
Sparse Core Ops, SparseCore 0:
  115.2 69.6 all-gather.2
  359.3 66.4 reduce-scatter.3
